TPU v7x, 256 devices: a whole 4x4x8 slice. The times are simulated.
256 devices in a mesh: var: 4 (over x), tok: 2 (over z_hi), mp: 32 (over z_lo, y, core).
Axes of the slice: x: 4, y: 4, z: 8 (z_hi: 2, z_lo: 4; z = z_hi * 4 + z_lo), core: 2. Of those that a mesh axis runs over, the one named last changes fastest.
Arguments:
- patches: bfloat16 [88, 32, 64], P('var', 'tok'), may hold values from -6 to 6
- embed_weight: bfloat16 [88, 64, 12288], P('var', None, 'mp'), may hold values from -0.75 to 0.75
- embed_bias: bfloat16 [88, 12288], P('var', 'mp'), may hold values from -3 to 3
- queries: bfloat16 [32, 12288], P('tok', 'mp'), may hold values from -6 to 6
- score_bias: float32 [32, 88], P('tok'), may hold values from -4 to 260
- key_weight: bfloat16 [32, 384, 12288], P(None, 'var', 'mp'), may hold values from -0.0546875 to 0.0546875
- value_weight: bfloat16 [32, 384, 12288], P(None, 'var', 'mp'), may hold values from -0.0546875 to 0.0546875
- out_weight: bfloat16 [12288, 12288], P('mp', 'var'), may hold values from -0.109375 to 0.109375
- out_bias: bfloat16 [12288], P(('var', 'mp')), may hold values from -3 to 3
Outputs:
- aggregated: bfloat16 [32, 12288], P('tok', ('var', 'mp'))
All inputs are finite; a program needn't handle non-finite values.
Results may differ from a plain program's by a relative error of at most 0.005.
Values may be sent and summed in bfloat16 or wider, within the bound.
No kernel may reach another device: no remote copies, remote signals or barrier semaphores. Data moves between devices by JAX's collectives and lax.ppermute only.
A program may use at most 128 MiB of HBM per device.

v0:
```python
import functools
import math

import jax
import jax.numpy as jnp
import numpy as np
from jax import lax
from jax.experimental import pallas as pl
from jax.experimental.pallas import tpu as pltpu
from jax.sharding import PartitionSpec as P

HD = 384
Z, Y, C = 4, 4, 2
STEPS = (2, 1, 3, 0)
COST = 2**16
VMEM = 8 * 2**20


def move(array, there):
    pairs = []
    for z in range(Z):
        for y in range(Y):
            for c in range(C):
                z2, y2, c2 = there(z, y, c)
                pairs.append(((z * Y + y) * C + c, ((z2 % Z) * Y + y2 % Y) * C + c2 % C))
    return lax.ppermute(array, "mp", pairs)


def other_core(array):
    return move(array, lambda z, y, c: (z, y, 1 - c))


def along_z(array, step):
    return move(array, lambda z, y, c: (z + step, y, c))


def along_y(array):
    return move(array, lambda z, y, c: (z, y + 1 - 2 * c, c))


def local_call(
    kernel, after, arrays, specs, out_shape, out_block, name, dtype=jnp.bfloat16
):
    return pl.pallas_call(
        kernel,
        grid=(1,),
        in_specs=[pl.BlockSpec(memory_space=pl.ANY)] + specs,
        out_specs=out_block,
        out_shape=jax.ShapeDtypeStruct(out_shape, dtype),
        compiler_params=pltpu.CompilerParams(vmem_limit_bytes=VMEM),
        cost_estimate=pl.CostEstimate(flops=0, transcendentals=0, bytes_accessed=COST),
        name=name,
    )(after, *arrays)


def copy_kernel(after, array, out):
    if len(out.shape) == 2 and out.shape[0] % 16 == 0:

        @pl.loop(0, out.shape[0] // 16)
        def _(n):
            rows = pl.ds(pl.multiple_of(n * 16, 16), 16)
            out[rows, :] = array[rows, :]

    else:
        out[...] = array[...]


def pack_kernel(first, groups, after, received, out):
    owners, width = received.shape[0], received.shape[3]

    @pl.loop(0, out.shape[0])
    def _(chunk):
        for owner in range(owners):
            out[chunk, :, owner * width : (owner + 1) * width] = received[
                owner, groups[first + chunk]
            ]


def pack(received, groups, first, count, after):
    owners, _, rows, width = received.shape
    return pl.pallas_call(
        functools.partial(pack_kernel, first),
        in_specs=[
            pl.BlockSpec(memory_space=pltpu.SMEM),
            pl.BlockSpec(memory_space=pl.ANY),
            pl.BlockSpec(memory_space=pltpu.VMEM),
        ],
        out_specs=pl.BlockSpec(memory_space=pltpu.VMEM),
        out_shape=jax.ShapeDtypeStruct((count, rows, owners * width), jnp.bfloat16),
        compiler_params=pltpu.CompilerParams(vmem_limit_bytes=VMEM),
        cost_estimate=pl.CostEstimate(flops=0, transcendentals=0, bytes_accessed=COST),
        name="pack",
    )(groups, after, received)


def first_half(array, after):
    rows, width = array.shape
    block = pl.BlockSpec((rows, width // 2), lambda k: (0, 0))
    return local_call(copy_kernel, after, [array], [block], (rows, width // 2), block, "half")


def line_kernel(chunk, first, second, *refs):
    *parts, out, wide = refs
    tile = out.shape[1] // len(parts)
    rows = parts[0].shape[1]
    for n, part in enumerate(parts):
        values = part[chunk].astype(jnp.float32)
        for block in range(values.shape[1] // tile):
            wide[block * rows : (block + 1) * rows, n * tile : (n + 1) * tile] = values[
                :, block * tile : (block + 1) * tile
            ]

    @pl.loop(0, out.shape[0] // 16)
    def _(n):
        group = pl.ds(pl.multiple_of(n * 16, 16), 16)
        out[group, :] = wide[group, :].astype(out.dtype)


def line_of(parts, chunk, *after):
    _, rows, width = parts[0].shape
    tile = width // 4
    shape = (rows * 4, tile * len(parts))
    return pl.pallas_call(
        functools.partial(line_kernel, chunk),
        in_specs=[pl.BlockSpec(memory_space=pl.ANY)] * 2
        + [pl.BlockSpec(memory_space=pltpu.VMEM) for _ in parts],
        out_specs=pl.BlockSpec(memory_space=pltpu.VMEM),
        out_shape=jax.ShapeDtypeStruct(shape, jnp.bfloat16),
        scratch_shapes=[pltpu.VMEM(shape, jnp.float32)],
        compiler_params=pltpu.CompilerParams(vmem_limit_bytes=VMEM),
        cost_estimate=pl.CostEstimate(flops=0, transcendentals=0, bytes_accessed=COST),
        name="line",
    )(*after, *parts)


def copied(array, after):
    block = pl.BlockSpec(array.shape, lambda k: (0,) * array.ndim)
    return local_call(
        copy_kernel, after, [array], [block], array.shape, block, "copied", array.dtype
    )


def order_kernel(order, keys, values, *refs):
    *outs, done, held, sems, out_sems = refs
    done[...] = jnp.zeros_like(done)
    width = keys.shape[2]

    def copies(n):
        return [
            pltpu.make_async_copy(
                weight.at[order[n]], held.at[n, :, pl.ds(k * width, width)], sems.at[k, n]
            )
            for k, weight in enumerate((keys, values))
        ]

    @pl.loop(0, keys.shape[0])
    def _(n):
        for copy in copies(n):
            copy.start()

    leaving = []
    first = 0
    for m, out in enumerate(outs):
        last = first + out.shape[0]

        @pl.loop(first, last)
        def _(n):
            for copy in copies(n):
                copy.wait()

        leaving.append(
            pltpu.make_async_copy(held.at[pl.ds(first, last - first)], out, out_sems.at[m])
        )
        leaving[-1].start()
        first = last
    for copy in leaving:
        copy.wait()


def ordered_weights(order, keys, values, counts):
    tiles, rows, width = keys.shape
    anywhere = pl.BlockSpec(memory_space=pl.ANY)
    return pl.pallas_call(
        order_kernel,
        in_specs=[pl.BlockSpec(memory_space=pltpu.SMEM), anywhere, anywhere],
        out_specs=[pl.BlockSpec(memory_space=pltpu.HBM) for _ in counts]
        + [pl.BlockSpec(memory_space=pltpu.VMEM)],
        out_shape=[pltpu.HBM((n, rows, 2 * width), keys.dtype) for n in counts]
        + [jax.ShapeDtypeStruct((8, 128), jnp.float32)],
        scratch_shapes=[
            pltpu.VMEM((tiles, rows, 2 * width), keys.dtype),
            pltpu.SemaphoreType.DMA((2, tiles)),
            pltpu.SemaphoreType.DMA((len(counts),)),
        ],
        compiler_params=pltpu.CompilerParams(vmem_limit_bytes=VMEM),
        cost_estimate=pl.CostEstimate(flops=0, transcendentals=0, bytes_accessed=10 * 2**20),
        name="order_weights",
    )(order, keys, values)


def arrival_order(ids):
    def sent(ids, there):
        result = np.zeros_like(ids)
        for n in range(Z * Y * C):
            z, y, c = there(n // (Y * C), n // C % Y, n % C)
            result[(z % Z * Y + y % Y) * C + c % C] = ids[n]
        return result

    def up_or_down(ids):
        return sent(ids, lambda z, y, c: (z, y + 1 - 2 * c, c))

    def swapped(ids):
        return sent(ids, lambda z, y, c: (z, y, 1 - c))

    mine = [ids] + [sent(ids, lambda z, y, c: (z + step, y, c)) for step in (1, 3, 2)]
    line = np.concatenate(mine + [swapped(part) for part in mine], axis=1)
    near = up_or_down(line)
    far = up_or_down(near[:, : near.shape[1] // 2])
    return np.concatenate([line, near, swapped(near), far, swapped(far)], axis=1)


def core_var_shift(array):
    n = lax.axis_size("var")
    m = lax.axis_size("mp")
    pairs = [
        (k * m + p, (k + 1 - 2 * (p % C)) % n * m + p) for k in range(n) for p in range(m)
    ]
    return lax.ppermute(array, ("var", "mp"), pairs)


def var_shift(array, step):
    n = lax.axis_size("var")
    return lax.ppermute(array, "var", [(k, (k + step) % n) for k in range(n)])


def on_device(
    patches,
    embed_weight,
    embed_bias,
    queries,
    score_bias,
    key_weight,
    value_weight,
    out_weight,
    out_bias,
):
    var_count = lax.axis_size("var")
    mp_count = lax.axis_size("mp")
    var_place = lax.axis_index("var")
    local_vars, tok_rows, _ = patches.shape
    all_vars = local_vars * var_count
    tile_width = embed_weight.shape[2]
    quarter = tile_width // var_count
    part_tokens = tok_rows // var_count
    rows = part_tokens * all_vars
    f32 = jnp.float32
    embedded = jnp.einsum("vtp,vpc->vtc", patches, embed_weight, preferred_element_type=f32)
    embedded = (embedded + embed_bias[:, None, :].astype(f32)).astype(jnp.bfloat16)
    own = embedded.reshape(local_vars, var_count, part_tokens, var_count, quarter)
    own = own.transpose(3, 1, 0, 2, 4).reshape(var_count, var_count, -1, quarter)
    order = arrival_order(np.arange(mp_count)[:, None])
    order = jnp.take(jnp.asarray(order, jnp.int32), lax.axis_index("mp"), axis=0)
    *weights, ordered = ordered_weights(order, key_weight, value_weight, (8, 8, 8, 4, 4))
    received = lax.all_to_all(own, "var", split_axis=0, concat_axis=0, tiled=True)
    groups = jnp.stack([(var_place + step) % var_count for step in STEPS]).astype(jnp.int32)
    weights = [w.reshape(-1, 2 * tile_width) for w in weights]
    early = pack(received, groups, 0, 2, ordered)
    late = pack(received, groups, 2, 2, early)
    early = [early] + [along_z(early, step) for step in (1, 3, 2)]
    late = [late] + [along_z(late, step) for step in (1, 3, 2)]
    early += [other_core(part) for part in early]

    def product(line, near, far):
        total = 0.0
        for part, weight in zip([line, near, other_core(near), far, other_core(far)], weights):
            total = total + jnp.dot(part, weight, preferred_element_type=f32)
        return total

    core = lax.axis_index("mp") % C
    line0 = line_of(early, 0, late[1], late[2])
    near0 = along_y(line0)
    line1 = line_of(early, 1, line0, line0)
    near1 = along_y(line1)
    half0 = first_half(near0, line1)
    far0 = along_y(half0)
    late[3] = copied(late[3], half0)
    late += [other_core(part) for part in late]
    half1 = first_half(near1, half0)
    far1 = along_y(half1)
    line2 = line_of(late, 0, half1, half1)
    near2 = along_y(line2)
    far0 = copied(far0, line2)
    far_sent = product(line0, near0, far0).astype(jnp.bfloat16)
    far = core_var_shift(far_sent).astype(f32)
    half2 = first_half(near2, far_sent)
    far2 = along_y(half2)
    line3 = line_of(late, 1, half2, half2)
    near3 = along_y(line3)
    far1 = copied(far1, line3)
    ahead_sent = product(line1, near1, far1) + jnp.where(core == 0, far, 0.0)
    ahead_sent = ahead_sent.astype(jnp.bfloat16)
    far2 = copied(far2, far1)
    behind_sent = product(line2, near2, far2) + jnp.where(core == 1, far, 0.0)
    behind_sent = behind_sent.astype(jnp.bfloat16)
    from_behind = var_shift(ahead_sent, 1)
    from_ahead = var_shift(behind_sent, -1)
    half3 = first_half(near3, behind_sent)
    far3 = along_y(half3)
    totals = product(line3, near3, far3)
    totals = totals + from_behind.astype(f32) + from_ahead.astype(f32)

    keys, values = totals[:, :tile_width], totals[:, tile_width:]
    scale = lax.rsqrt(jnp.mean(keys * keys, axis=1) + 1e-06)
    query_rows = lax.dynamic_slice_in_dim(
        copied(queries, behind_sent), var_place * part_tokens, part_tokens, 0)
    bias_rows = lax.dynamic_slice_in_dim(
        copied(score_bias, behind_sent), var_place * part_tokens, part_tokens, 0)
    token = np.arange(rows) % part_tokens
    spot = jnp.asarray(token[:, None] == np.arange(part_tokens))
    spread = jnp.dot(spot.astype(jnp.bfloat16), query_rows, preferred_element_type=f32)
    spread = lax.optimization_barrier(spread)
    scores = (spread * keys).sum(1) * scale / math.sqrt(HD) + bias_rows.T.reshape(rows)
    scores = jnp.where(spot, scores[:, None], -jnp.inf)
    weight = jnp.exp(scores - scores.max(0, keepdims=True))
    attention = weight / weight.sum(0, keepdims=True)
    mixed = lax.dot_general(
        attention, values, (((0,), (0,)), ((), ())), precision=lax.Precision.HIGHEST
    ).astype(jnp.bfloat16)

    every_token = jnp.zeros((tok_rows, tile_width), jnp.bfloat16)
    for step in (2, 1, 3, 0):
        piece = var_shift(mixed, step) if step else mixed
        place = (var_place - step) % var_count
        every_token = lax.dynamic_update_slice_in_dim(every_token, piece, place * part_tokens, 0)
    product = jnp.dot(every_token, out_weight, preferred_element_type=f32)
    product = product.astype(jnp.bfloat16).reshape(tok_rows, mp_count, -1).transpose(1, 0, 2)
    terms = lax.all_to_all(product, "mp", split_axis=0, concat_axis=0, tiled=True)
    summed = terms.astype(f32).sum(0)
    return (summed + out_bias.astype(f32)[None, :]).astype(jnp.bfloat16)


def solution(mesh):
    in_specs = (
        P("var", "tok", None),
        P("var", None, "mp"),
        P("var", "mp"),
        P("tok", "mp"),
        P("tok", None),
        P(None, "var", "mp"),
        P(None, "var", "mp"),
        P("mp", "var"),
        P(("var", "mp")),
    )
    out_specs = P("tok", ("var", "mp"))
    return jax.shard_map(
        on_device, mesh=mesh, in_specs=in_specs, out_specs=out_specs, check_vma=False
    )
```

profile of v0, /device:TPU:1, one launch (start us, length us, event | category | flops | bytes accessed | tf_op | source)
XLA Modules:
  0.0 127.4 jit_solution(16879278650261483)
XLA Ops:
  0.9 1.6 %fusion.18 = bf16[22,16,384]{2,1,0:T(8,128)(2,1)S(1)} fusion(bf16[22,16,64]{2,1,0:T(8,128)(2,1)} %param.11, bf16[22,64,384]{2,1,0:T(8,128)(2,1)} %param.12, f32[22,384]{1,0:T(8,128)S(1)} %convert_element_type.41), kind=kOutput, calls=%fused_computation.27 | convolution fusion | flops 17571840 | bytes 1430528 | tf_op jit(solution)/shard_map/vtp,vpc->vtc/dot_general | solution.py:257
  3.6 4.8 %all-to-all-start = ((bf16[4,4,88,96]{3,2,1,0:T(8,128)(2,1)}), bf16[4,4,88,96]{3,2,1,0:T(8,128)(2,1)S(1)}, u32[]{:S(2)}, u32[]{:S(2)}) async-start(bf16[4,4,88,96]{3,2,1,0:T(8,128)(2,1)} %bitcast.6), calls=%async_computation | async-start | bytes 720896 | tf_op jit(solution)/shard_map/all_to_all | solution.py:264
  9.2 1.7 %copy-done.3 = bf16[32,96,384]{2,1,0:T(8,128)(2,1)S(1)} copy-done((bf16[32,96,384]{2,1,0:T(8,128)(2,1)S(1)}, bf16[32,96,384]{2,1,0:T(8,128)(2,1)}, u32[]{:S(2)}) %copy-start.3) | copy-done | bytes 2359320
  10.8 1.7 %copy-done.4 = bf16[32,96,384]{2,1,0:T(8,128)(2,1)S(1)} copy-done((bf16[32,96,384]{2,1,0:T(8,128)(2,1)S(1)}, bf16[32,96,384]{2,1,0:T(8,128)(2,1)}, u32[]{:S(2)}) %copy-start.4) | copy-done | bytes 2359320
  12.5 4.3 %order_weights.1 = (bf16[8,96,768]{2,1,0:T(8,128)(2,1)}, bf16[8,96,768]{2,1,0:T(8,128)(2,1)}, bf16[8,96,768]{2,1,0:T(8,128)(2,1)}, bf16[4,96,768]{2,1,0:T(8,128)...) custom-call(s32[32]{0:T(128)S(1)} %fusion.31.order, bf16[32,96,384]{2,1,0:T(8,128)(2,1)S(1)} %copy-done.3, ...), custom_call_target="tpu_custom_call" | custom-call | bytes 10485760 | tf_op jit(solution)/shard_map/order_weights/pallas_call | solution.py:183
  17.6 1.7 %collective-permute-start.2 = (bf16[2,88,384]{2,1,0:T(8,128)(2,1)S(1)}, bf16[2,88,384]{2,1,0:T(8,128)(2,1)S(1)}, u32[]{:S(2)}, u32[]{:S(2)}) collective-permute-start(bf16[2,88,384]{2,1,0:T(8,128)(2,1)S(1)} %pack.2.after.refs_0_), channel_id=1, source_target_pairs={{0,8},{1,9},{2,10},{3,11},{4,12},{5,13},{6,14},{7,15},{8,16},{9,17... | collective-permute-start | bytes 405512 | tf_op jit(solution)/shard_map/ppermute | solution.py:26
  19.3 2.8 %collective-permute-start.3 = (bf16[2,88,384]{2,1,0:T(8,128)(2,1)S(1)}, bf16[2,88,384]{2,1,0:T(8,128)(2,1)S(1)}, u32[]{:S(2)}, u32[]{:S(2)}) collective-permute-start(bf16[2,88,384]{2,1,0:T(8,128)(2,1)S(1)} %pack.2.after.refs_0_), channel_id=1, source_target_pairs={{0,24},{1,25},{2,26},{3,27},{4,28},{5,29},{6,30},{7,31},{8,0},{9,1... | collective-permute-start | bytes 405512 | tf_op jit(solution)/shard_map/ppermute | solution.py:26
  23.1 1.5 %collective-permute-start = (bf16[2,88,384]{2,1,0:T(8,128)(2,1)S(1)}, bf16[2,88,384]{2,1,0:T(8,128)(2,1)S(1)}, u32[]{:S(2)}, u32[]{:S(2)}) collective-permute-start(bf16[2,88,384]{2,1,0:T(8,128)(2,1)S(1)} %pack.3.refs_0_), channel_id=1, source_target_pairs={{0,8},{1,9},{2,10},{3,11},{4,12},{5,13},{6,14},{7,15},{8,16},{9,17... | collective-permute-start | bytes 405512 | tf_op jit(solution)/shard_map/ppermute | solution.py:26
  24.6 1.8 %collective-permute-start.1 = (bf16[2,88,384]{2,1,0:T(8,128)(2,1)S(1)}, bf16[2,88,384]{2,1,0:T(8,128)(2,1)S(1)}, u32[]{:S(2)}, u32[]{:S(2)}) collective-permute-start(bf16[2,88,384]{2,1,0:T(8,128)(2,1)S(1)} %pack.3.refs_0_), channel_id=1, source_target_pairs={{0,24},{1,25},{2,26},{3,27},{4,28},{5,29},{6,30},{7,31},{8,0},{9,1... | collective-permute-start | bytes 405512 | tf_op jit(solution)/shard_map/ppermute | solution.py:26
  26.4 2.2 %collective-permute-start.5 = (bf16[2,88,384]{2,1,0:T(8,128)(2,1)S(1)}, bf16[2,88,384]{2,1,0:T(8,128)(2,1)S(1)}, u32[]{:S(2)}, u32[]{:S(2)}) collective-permute-start(bf16[2,88,384]{2,1,0:T(8,128)(2,1)S(1)} %pack.2.after.refs_0_), channel_id=1, source_target_pairs={{0,1},{1,0},{2,3},{3,2},{4,5},{5,4},{6,7},{7,6},{8,9},{9,8},{10,11... | collective-permute-start | bytes 405512 | tf_op jit(solution)/shard_map/ppermute | solution.py:26
  28.9 8.7 %collective-permute-done.4.refs_3_ = bf16[2,88,384]{2,1,0:T(8,128)(2,1)S(1)} collective-permute-done((bf16[2,88,384]{2,1,0:T(8,128)(2,1)S(1)}, bf16[2,88,384]{2,1,0:T(8,128)(2,1)S(1)}, u32[]{:S(2)}, u32[]{:S(2)}) %collective-permute-start.4) | collective-permute-done | bytes 135200 | tf_op jit(solution)/shard_map/ppermute | solution.py:26
  40.1 2.8 %collective-permute-start.9 = (bf16[352,768]{1,0:T(8,128)(2,1)S(1)}, bf16[352,768]{1,0:T(8,128)(2,1)}, u32[]{:S(2)}, u32[]{:S(2)}) collective-permute-start(bf16[352,768]{1,0:T(8,128)(2,1)S(1)} %line.4.first.second), channel_id=1, source_target_pairs={{0,2},{1,7},{2,4},{3,1},{4,6},{5,3},{6,0},{7,5},{8,10},{9,15},{10,... | collective-permute-start | bytes 1622024 | tf_op jit(solution)/shard_map/ppermute | solution.py:26
  43.9 2.5 %collective-permute-start.11 = (bf16[2,88,384]{2,1,0:T(8,128)(2,1)}, bf16[2,88,384]{2,1,0:T(8,128)(2,1)S(1)}, u32[]{:S(2)}, u32[]{:S(2)}) collective-permute-start(bf16[2,88,384]{2,1,0:T(8,128)(2,1)} %copy-done.5), channel_id=1, source_target_pairs={{0,16},{1,17},{2,18},{3,19},{4,20},{5,21},{6,22},{7,23},{8,24},{9,... | collective-permute-start | bytes 405512 | tf_op jit(solution)/shard_map/ppermute | solution.py:26
  47.0 2.2 %collective-permute-done.9.array = bf16[352,768]{1,0:T(8,128)(2,1)} collective-permute-done((bf16[352,768]{1,0:T(8,128)(2,1)S(1)}, bf16[352,768]{1,0:T(8,128)(2,1)}, u32[]{:S(2)}, u32[]{:S(2)}) %collective-permute-start.9) | collective-permute-done | bytes 540704 | tf_op jit(solution)/shard_map/ppermute | solution.py:26
  49.2 1.8 %collective-permute-start.14 = (bf16[2,88,384]{2,1,0:T(8,128)(2,1)}, bf16[2,88,384]{2,1,0:T(8,128)(2,1)S(1)}, u32[]{:S(2)}, u32[]{:S(2)}) collective-permute-start(bf16[2,88,384]{2,1,0:T(8,128)(2,1)} %copy-done.9), channel_id=1, source_target_pairs={{0,1},{1,0},{2,3},{3,2},{4,5},{5,4},{6,7},{7,6},{8,9},{9,8},{10,11... | collective-permute-start | bytes 405512 | tf_op jit(solution)/shard_map/ppermute | solution.py:26
  51.0 2.0 %fusion.35 = f32[352,768]{1,0:T(8,128)S(1)} fusion(bf16[352,768]{1,0:T(8,128)(2,1)} %collective-permute-done.9.array, bf16[768,768]{1,0:T(8,128)(2,1)} %bitcast.72), kind=kOutput, calls=%fused_computation.60 | convolution fusion | flops 415236096 | bytes 2801664 | tf_op jit(solution)/shard_map/dot_general | solution.py:276
  54.2 1.8 %collective-permute-start.19 = (bf16[352,384]{1,0:T(8,128)(2,1)S(1)}, bf16[352,384]{1,0:T(8,128)(2,1)S(1)}, u32[]{:S(2)}, u32[]{:S(2)}) collective-permute-start(bf16[352,384]{1,0:T(8,128)(2,1)S(1)} %half.4.after), channel_id=1, source_target_pairs={{0,2},{1,7},{2,4},{3,1},{4,6},{5,3},{6,0},{7,5},{8,10},{9,15},{10,... | collective-permute-start | bytes 811016 | tf_op jit(solution)/shard_map/ppermute | solution.py:26
  56.8 1.6 %fusion.44 = f32[352,768]{1,0:T(8,128)S(1)} fusion(bf16[352,768]{1,0:T(8,128)(2,1)} %collective-permute-done.10.array, bf16[768,768]{1,0:T(8,128)(2,1)S(1)} %bitcast.74), kind=kOutput, calls=%fused_computation.69 | convolution fusion | flops 415236096 | bytes 2801664 | tf_op jit(solution)/shard_map/dot_general | solution.py:276
  59.6 1.6 %collective-permute-start.21 = (bf16[352,384]{1,0:T(8,128)(2,1)S(1)}, bf16[352,384]{1,0:T(8,128)(2,1)S(1)}, u32[]{:S(2)}, u32[]{:S(2)}) collective-permute-start(bf16[352,384]{1,0:T(8,128)(2,1)S(1)} %half.5.first.second), channel_id=1, source_target_pairs={{0,2},{1,7},{2,4},{3,1},{4,6},{5,3},{6,0},{7,5},{8,10},{9,15},{10,... | collective-permute-start | bytes 811016 | tf_op jit(solution)/shard_map/ppermute | solution.py:26
  67.1 3.0 %collective-permute-start.24 = (bf16[352,768]{1,0:T(8,128)(2,1)S(1)}, bf16[352,768]{1,0:T(8,128)(2,1)S(1)}, u32[]{:S(2)}, u32[]{:S(2)}) collective-permute-start(bf16[352,768]{1,0:T(8,128)(2,1)S(1)} %fusion.17.after), channel_id=1, source_target_pairs={{0,64},{1,193},{2,66},{3,195},{4,68},{5,197},{6,70},{7,199},{8,72}... | collective-permute-start | bytes 1622024 | tf_op jit(solution)/shard_map/ppermute | solution.py:228
  71.2 2.8 %collective-permute-start.22 = (bf16[352,384]{1,0:T(8,128)(2,1)S(1)}, bf16[352,384]{1,0:T(8,128)(2,1)S(1)}, u32[]{:S(2)}, u32[]{:S(2)}) collective-permute-start(bf16[352,384]{1,0:T(8,128)(2,1)S(1)} %half.6.first.second), channel_id=1, source_target_pairs={{0,2},{1,7},{2,4},{3,1},{4,6},{5,3},{6,0},{7,5},{8,10},{9,15},{10,... | collective-permute-start | bytes 811016 | tf_op jit(solution)/shard_map/ppermute | solution.py:26
  77.5 3.9 %collective-permute-start.23 = (bf16[352,384]{1,0:T(8,128)(2,1)S(1)}, bf16[352,384]{1,0:T(8,128)(2,1)S(1)}, u32[]{:S(2)}, u32[]{:S(2)}) collective-permute-start(bf16[352,384]{1,0:T(8,128)(2,1)S(1)} %copied.9), channel_id=1, source_target_pairs={{0,1},{1,0},{2,3},{3,2},{4,5},{5,4},{6,7},{7,6},{8,9},{9,8},{10,11... | collective-permute-start | bytes 811016 | tf_op jit(solution)/shard_map/ppermute | solution.py:26
  82.4 1.5 %fusion.16 = bf16[352,768]{1,0:T(8,128)(2,1)} fusion(f32[352,768]{1,0:T(8,128)S(1)} %fusion.47, f32[352,768]{1,0:T(8,128)S(1)} %fusion.46, f32[352,768]{1,0:T(8,128)S(1)} %fusion.45, f32[352,768]{1,0:T(8,128)S(1)} %fusion.44, bf16[352,768]{1,0:T(8,128)(2,1)S(1)} %line.5.after, bf16[768,768]{1,0:T(8,128)(2,1)S(1)} %bitcast.65, ...), kind=kOutput, calls=%fused_computation.24 | convolution fusion | flops 417398784 | bytes 7127041 | tf_op jit(solution)/shard_map/dot_general | solution.py:276
  83.9 1.7 %collective-permute-start.31 = (bf16[352,768]{1,0:T(8,128)(2,1)}, bf16[352,768]{1,0:T(8,128)(2,1)}, u32[]{:S(2)}, u32[]{:S(2)}) collective-permute-start(bf16[352,768]{1,0:T(8,128)(2,1)} %fusion.16), channel_id=1, source_target_pairs={{0,64},{64,128},{128,192},{192,0},{1,65},{65,129},{129,193},{193,1... | collective-permute-start | bytes 1622024 | tf_op jit(solution)/shard_map/ppermute | solution.py:233
  91.3 1.9 %fusion.41 = f32[352,768]{1,0:T(8,128)S(1)} fusion(bf16[352,768]{1,0:T(8,128)(2,1)S(1)} %collective-permute-done.25.array, bf16[768,768]{1,0:T(8,128)(2,1)} %bitcast.73), kind=kOutput, calls=%fused_computation.66 | convolution fusion | flops 415236096 | bytes 2801664 | tf_op jit(solution)/shard_map/dot_general | solution.py:276
  93.2 2.3 %collective-permute-done.27 = bf16[352,384]{1,0:T(8,128)(2,1)} collective-permute-done((bf16[352,384]{1,0:T(8,128)(2,1)}, bf16[352,384]{1,0:T(8,128)(2,1)}, u32[]{:S(2)}, u32[]{:S(2)}) %collective-permute-start.27) | collective-permute-done | bytes 270368 | tf_op jit(solution)/shard_map/ppermute | solution.py:26
  95.5 2.4 %collective-permute-start.28 = (bf16[352,384]{1,0:T(8,128)(2,1)}, bf16[352,384]{1,0:T(8,128)(2,1)S(1)}, u32[]{:S(2)}, u32[]{:S(2)}) collective-permute-start(bf16[352,384]{1,0:T(8,128)(2,1)} %collective-permute-done.27), channel_id=1, source_target_pairs={{0,1},{1,0},{2,3},{3,2},{4,5},{5,4},{6,7},{7,6},{8,9},{9,8},{10,11... | collective-permute-start | bytes 811016 | tf_op jit(solution)/shard_map/ppermute | solution.py:26
  101.8 1.7 %fusion.5 = f32[352,768]{1,0:T(8,128)S(1)} fusion(f32[352,768]{1,0:T(8,128)S(1)} %fusion.7, bf16[352,384]{1,0:T(8,128)(2,1)S(1)} %collective-permute-done.28, bf16[384,768]{1,0:T(8,128)(2,1)S(1)} %bitcast.79, bf16[352,768]{1,0:T(8,128)(2,1)} %collective-permute-done.32, bf16[352,768]{1,0:T(8,128)(2,1)} %collective-permute-done.31), kind=kOutput, calls=%fused_computation.8 | convolution fusion | flops 208969728 | bytes 4104192 | tf_op jit(solution)/shard_map/dot_general | solution.py:276
  104.4 2.1 %collective-permute-start.33 = (bf16[4,384]{1,0:T(4,128)(2,1)S(1)}, bf16[4,384]{1,0:T(4,128)(2,1)S(1)}, u32[]{:S(2)}, u32[]{:S(2)}) collective-permute-start(bf16[4,384]{1,0:T(4,128)(2,1)S(1)} %convolution_convert_fusion.1), channel_id=1, source_target_pairs={{0,128},{64,192},{128,0},{192,64},{1,129},{65,193},{129,1},{193,65... | collective-permute-start | bytes 9224 | tf_op jit(solution)/shard_map/ppermute | solution.py:233
  107.1 2.0 %collective-permute-start.35 = (bf16[4,384]{1,0:T(4,128)(2,1)S(1)}, bf16[4,384]{1,0:T(4,128)(2,1)S(1)}, u32[]{:S(2)}, u32[]{:S(2)}) collective-permute-start(bf16[4,384]{1,0:T(4,128)(2,1)S(1)} %convolution_convert_fusion.1), channel_id=1, source_target_pairs={{0,192},{64,0},{128,64},{192,128},{1,193},{65,1},{129,65},{193,129... | collective-permute-start | bytes 9224 | tf_op jit(solution)/shard_map/ppermute | solution.py:233
  111.5 6.7 %all-to-all-start.1 = ((bf16[32,16,96]{2,1,0:T(8,128)(2,1)}), bf16[32,16,96]{2,1,0:T(8,128)(2,1)S(1)}, u32[]{:S(2)}, u32[]{:S(2)}) async-start(bf16[32,16,96]{2,1,0:T(8,128)(2,1)} %bitcast.63), calls=%async_computation.1 | async-start | bytes 262144 | tf_op jit(solution)/shard_map/all_to_all | solution.py:337
  118.3 8.5 %all-to-all-done.1 = bf16[32,16,96]{2,1,0:T(8,128)(2,1)S(1)} async-done(((bf16[32,16,96]{2,1,0:T(8,128)(2,1)}), bf16[32,16,96]{2,1,0:T(8,128)(2,1)S(1)}, u32[]{:S(2)}, u32[]{:S(2)}) %all-to-all-start.1) | async-done | bytes 98336 | tf_op jit(solution)/shard_map/all_to_all | solution.py:337
  (157 shorter events, 37.1 us)
Async XLA Ops:
  3.6 13.2 %all-to-all-start = ((bf16[4,4,88,96]{3,2,1,0:T(8,128)(2,1)}), bf16[4,4,88,96]{3,2,1,0:T(8,128)(2,1)S(1)}, u32[]{:S(2)}, u32[]{:S(2)}) async-start(bf16[4,4,88,96]{3,2,1,0:T(8,128)(2,1)} %bitcast.6), calls=%async_computation | async-start | bytes 720896 | tf_op jit(solution)/shard_map/all_to_all | solution.py:264
  17.6 8.8 %collective-permute-start.2 = (bf16[2,88,384]{2,1,0:T(8,128)(2,1)S(1)}, bf16[2,88,384]{2,1,0:T(8,128)(2,1)S(1)}, u32[]{:S(2)}, u32[]{:S(2)}) collective-permute-start(bf16[2,88,384]{2,1,0:T(8,128)(2,1)S(1)} %pack.2.after.refs_0_), channel_id=1, source_target_pairs={{0,8},{1,9},{2,10},{3,11},{4,12},{5,13},{6,14},{7,15},{8,16},{9,17... | collective-permute-start | bytes 405512 | tf_op jit(solution)/shard_map/ppermute | solution.py:26
  19.3 9.3 %collective-permute-start.3 = (bf16[2,88,384]{2,1,0:T(8,128)(2,1)S(1)}, bf16[2,88,384]{2,1,0:T(8,128)(2,1)S(1)}, u32[]{:S(2)}, u32[]{:S(2)}) collective-permute-start(bf16[2,88,384]{2,1,0:T(8,128)(2,1)S(1)} %pack.2.after.refs_0_), channel_id=1, source_target_pairs={{0,24},{1,25},{2,26},{3,27},{4,28},{5,29},{6,30},{7,31},{8,0},{9,1... | collective-permute-start | bytes 405512 | tf_op jit(solution)/shard_map/ppermute | solution.py:26
  22.1 15.5 %collective-permute-start.4 = (bf16[2,88,384]{2,1,0:T(8,128)(2,1)S(1)}, bf16[2,88,384]{2,1,0:T(8,128)(2,1)S(1)}, u32[]{:S(2)}, u32[]{:S(2)}) collective-permute-start(bf16[2,88,384]{2,1,0:T(8,128)(2,1)S(1)} %pack.2.after.refs_0_), channel_id=1, source_target_pairs={{0,16},{1,17},{2,18},{3,19},{4,20},{5,21},{6,22},{7,23},{8,24},{9,... | collective-permute-start | bytes 405512 | tf_op jit(solution)/shard_map/ppermute | solution.py:26
  23.1 15.2 %collective-permute-start = (bf16[2,88,384]{2,1,0:T(8,128)(2,1)S(1)}, bf16[2,88,384]{2,1,0:T(8,128)(2,1)S(1)}, u32[]{:S(2)}, u32[]{:S(2)}) collective-permute-start(bf16[2,88,384]{2,1,0:T(8,128)(2,1)S(1)} %pack.3.refs_0_), channel_id=1, source_target_pairs={{0,8},{1,9},{2,10},{3,11},{4,12},{5,13},{6,14},{7,15},{8,16},{9,17... | collective-permute-start | bytes 405512 | tf_op jit(solution)/shard_map/ppermute | solution.py:26
  24.6 13.8 %collective-permute-start.1 = (bf16[2,88,384]{2,1,0:T(8,128)(2,1)S(1)}, bf16[2,88,384]{2,1,0:T(8,128)(2,1)S(1)}, u32[]{:S(2)}, u32[]{:S(2)}) collective-permute-start(bf16[2,88,384]{2,1,0:T(8,128)(2,1)S(1)} %pack.3.refs_0_), channel_id=1, source_target_pairs={{0,24},{1,25},{2,26},{3,27},{4,28},{5,29},{6,30},{7,31},{8,0},{9,1... | collective-permute-start | bytes 405512 | tf_op jit(solution)/shard_map/ppermute | solution.py:26
  26.4 11.9 %collective-permute-start.5 = (bf16[2,88,384]{2,1,0:T(8,128)(2,1)S(1)}, bf16[2,88,384]{2,1,0:T(8,128)(2,1)S(1)}, u32[]{:S(2)}, u32[]{:S(2)}) collective-permute-start(bf16[2,88,384]{2,1,0:T(8,128)(2,1)S(1)} %pack.2.after.refs_0_), channel_id=1, source_target_pairs={{0,1},{1,0},{2,3},{3,2},{4,5},{5,4},{6,7},{7,6},{8,9},{9,8},{10,11... | collective-permute-start | bytes 405512 | tf_op jit(solution)/shard_map/ppermute | solution.py:26
  28.6 9.8 %collective-permute-start.6 = (bf16[2,88,384]{2,1,0:T(8,128)(2,1)S(1)}, bf16[2,88,384]{2,1,0:T(8,128)(2,1)S(1)}, u32[]{:S(2)}, u32[]{:S(2)}) collective-permute-start(bf16[2,88,384]{2,1,0:T(8,128)(2,1)S(1)} %collective-permute-done.2.refs_1_), channel_id=1, source_target_pairs={{0,1},{1,0},{2,3},{3,2},{4,5},{5,4},{6,7},{7,6},{8,9},{9,8},{10,11... | collective-permute-start | bytes 405512 | tf_op jit(solution)/shard_map/ppermute | solution.py:26
  40.1 9.1 %collective-permute-start.9 = (bf16[352,768]{1,0:T(8,128)(2,1)S(1)}, bf16[352,768]{1,0:T(8,128)(2,1)}, u32[]{:S(2)}, u32[]{:S(2)}) collective-permute-start(bf16[352,768]{1,0:T(8,128)(2,1)S(1)} %line.4.first.second), channel_id=1, source_target_pairs={{0,2},{1,7},{2,4},{3,1},{4,6},{5,3},{6,0},{7,5},{8,10},{9,15},{10,... | collective-permute-start | bytes 1622024 | tf_op jit(solution)/shard_map/ppermute | solution.py:26
  43.3 12.8 %collective-permute-start.10 = (bf16[352,768]{1,0:T(8,128)(2,1)S(1)}, bf16[352,768]{1,0:T(8,128)(2,1)}, u32[]{:S(2)}, u32[]{:S(2)}) collective-permute-start(bf16[352,768]{1,0:T(8,128)(2,1)S(1)} %line.5.after), channel_id=1, source_target_pairs={{0,2},{1,7},{2,4},{3,1},{4,6},{5,3},{6,0},{7,5},{8,10},{9,15},{10,... | collective-permute-start | bytes 1622024 | tf_op jit(solution)/shard_map/ppermute | solution.py:26
  43.9 10.3 %collective-permute-start.11 = (bf16[2,88,384]{2,1,0:T(8,128)(2,1)}, bf16[2,88,384]{2,1,0:T(8,128)(2,1)S(1)}, u32[]{:S(2)}, u32[]{:S(2)}) collective-permute-start(bf16[2,88,384]{2,1,0:T(8,128)(2,1)} %copy-done.5), channel_id=1, source_target_pairs={{0,16},{1,17},{2,18},{3,19},{4,20},{5,21},{6,22},{7,23},{8,24},{9,... | collective-permute-start | bytes 405512 | tf_op jit(solution)/shard_map/ppermute | solution.py:26
  46.4 9.6 %collective-permute-start.12 = (bf16[2,88,384]{2,1,0:T(8,128)(2,1)}, bf16[2,88,384]{2,1,0:T(8,128)(2,1)S(1)}, u32[]{:S(2)}, u32[]{:S(2)}) collective-permute-start(bf16[2,88,384]{2,1,0:T(8,128)(2,1)} %copy-done.5), channel_id=1, source_target_pairs={{0,1},{1,0},{2,3},{3,2},{4,5},{5,4},{6,7},{7,6},{8,9},{9,8},{10,11... | collective-permute-start | bytes 405512 | tf_op jit(solution)/shard_map/ppermute | solution.py:26
  47.0 12.6 %collective-permute-start.13 = (bf16[2,88,384]{2,1,0:T(8,128)(2,1)}, bf16[2,88,384]{2,1,0:T(8,128)(2,1)S(1)}, u32[]{:S(2)}, u32[]{:S(2)}) collective-permute-start(bf16[2,88,384]{2,1,0:T(8,128)(2,1)} %copy-done.7), channel_id=1, source_target_pairs={{0,1},{1,0},{2,3},{3,2},{4,5},{5,4},{6,7},{7,6},{8,9},{9,8},{10,11... | collective-permute-start | bytes 405512 | tf_op jit(solution)/shard_map/ppermute | solution.py:26
  49.2 12.0 %collective-permute-start.14 = (bf16[2,88,384]{2,1,0:T(8,128)(2,1)}, bf16[2,88,384]{2,1,0:T(8,128)(2,1)S(1)}, u32[]{:S(2)}, u32[]{:S(2)}) collective-permute-start(bf16[2,88,384]{2,1,0:T(8,128)(2,1)} %copy-done.9), channel_id=1, source_target_pairs={{0,1},{1,0},{2,3},{3,2},{4,5},{5,4},{6,7},{7,6},{8,9},{9,8},{10,11... | collective-permute-start | bytes 405512 | tf_op jit(solution)/shard_map/ppermute | solution.py:26
  54.2 9.0 %collective-permute-start.19 = (bf16[352,384]{1,0:T(8,128)(2,1)S(1)}, bf16[352,384]{1,0:T(8,128)(2,1)S(1)}, u32[]{:S(2)}, u32[]{:S(2)}) collective-permute-start(bf16[352,384]{1,0:T(8,128)(2,1)S(1)} %half.4.after), channel_id=1, source_target_pairs={{0,2},{1,7},{2,4},{3,1},{4,6},{5,3},{6,0},{7,5},{8,10},{9,15},{10,... | collective-permute-start | bytes 811016 | tf_op jit(solution)/shard_map/ppermute | solution.py:26
  56.0 5.2 %collective-permute-start.15 = (bf16[2,88,384]{2,1,0:T(8,128)(2,1)S(1)}, bf16[2,88,384]{2,1,0:T(8,128)(2,1)S(1)}, u32[]{:S(2)}, u32[]{:S(2)}) collective-permute-start(bf16[2,88,384]{2,1,0:T(8,128)(2,1)S(1)} %copied.6.refs_3_), channel_id=1, source_target_pairs={{0,1},{1,0},{2,3},{3,2},{4,5},{5,4},{6,7},{7,6},{8,9},{9,8},{10,11... | collective-permute-start | bytes 405512 | tf_op jit(solution)/shard_map/ppermute | solution.py:26
  56.1 7.8 %collective-permute-start.18 = (bf16[352,768]{1,0:T(8,128)(2,1)}, bf16[352,768]{1,0:T(8,128)(2,1)S(1)}, u32[]{:S(2)}, u32[]{:S(2)}) collective-permute-start(bf16[352,768]{1,0:T(8,128)(2,1)} %collective-permute-done.9.array), channel_id=1, source_target_pairs={{0,1},{1,0},{2,3},{3,2},{4,5},{5,4},{6,7},{7,6},{8,9},{9,8},{10,11... | collective-permute-start | bytes 1622024 | tf_op jit(solution)/shard_map/ppermute | solution.py:26
  59.6 15.0 %collective-permute-start.21 = (bf16[352,384]{1,0:T(8,128)(2,1)S(1)}, bf16[352,384]{1,0:T(8,128)(2,1)S(1)}, u32[]{:S(2)}, u32[]{:S(2)}) collective-permute-start(bf16[352,384]{1,0:T(8,128)(2,1)S(1)} %half.5.first.second), channel_id=1, source_target_pairs={{0,2},{1,7},{2,4},{3,1},{4,6},{5,3},{6,0},{7,5},{8,10},{9,15},{10,... | collective-permute-start | bytes 811016 | tf_op jit(solution)/shard_map/ppermute | solution.py:26
  61.2 8.9 %collective-permute-start.29 = (bf16[352,768]{1,0:T(8,128)(2,1)}, bf16[352,768]{1,0:T(8,128)(2,1)S(1)}, u32[]{:S(2)}, u32[]{:S(2)}) collective-permute-start(bf16[352,768]{1,0:T(8,128)(2,1)} %collective-permute-done.10.array), channel_id=1, source_target_pairs={{0,1},{1,0},{2,3},{3,2},{4,5},{5,4},{6,7},{7,6},{8,9},{9,8},{10,11... | collective-permute-start | bytes 1622024 | tf_op jit(solution)/shard_map/ppermute | solution.py:26
  61.7 9.4 %collective-permute-start.16 = (bf16[352,768]{1,0:T(8,128)(2,1)S(1)}, bf16[352,768]{1,0:T(8,128)(2,1)S(1)}, u32[]{:S(2)}, u32[]{:S(2)}) collective-permute-start(bf16[352,768]{1,0:T(8,128)(2,1)S(1)} %line.6.after), channel_id=1, source_target_pairs={{0,2},{1,7},{2,4},{3,1},{4,6},{5,3},{6,0},{7,5},{8,10},{9,15},{10,... | collective-permute-start | bytes 1622024 | tf_op jit(solution)/shard_map/ppermute | solution.py:26
  67.1 15.2 %collective-permute-start.24 = (bf16[352,768]{1,0:T(8,128)(2,1)S(1)}, bf16[352,768]{1,0:T(8,128)(2,1)S(1)}, u32[]{:S(2)}, u32[]{:S(2)}) collective-permute-start(bf16[352,768]{1,0:T(8,128)(2,1)S(1)} %fusion.17.after), channel_id=1, source_target_pairs={{0,64},{1,193},{2,66},{3,195},{4,68},{5,197},{6,70},{7,199},{8,72}... | collective-permute-start | bytes 1622024 | tf_op jit(solution)/shard_map/ppermute | solution.py:228
  71.2 6.2 %collective-permute-start.22 = (bf16[352,384]{1,0:T(8,128)(2,1)S(1)}, bf16[352,384]{1,0:T(8,128)(2,1)S(1)}, u32[]{:S(2)}, u32[]{:S(2)}) collective-permute-start(bf16[352,384]{1,0:T(8,128)(2,1)S(1)} %half.6.first.second), channel_id=1, source_target_pairs={{0,2},{1,7},{2,4},{3,1},{4,6},{5,3},{6,0},{7,5},{8,10},{9,15},{10,... | collective-permute-start | bytes 811016 | tf_op jit(solution)/shard_map/ppermute | solution.py:26
  74.5 14.2 %collective-permute-start.25 = (bf16[352,768]{1,0:T(8,128)(2,1)S(1)}, bf16[352,768]{1,0:T(8,128)(2,1)S(1)}, u32[]{:S(2)}, u32[]{:S(2)}) collective-permute-start(bf16[352,768]{1,0:T(8,128)(2,1)S(1)} %line.7.after), channel_id=1, source_target_pairs={{0,2},{1,7},{2,4},{3,1},{4,6},{5,3},{6,0},{7,5},{8,10},{9,15},{10,... | collective-permute-start | bytes 1622024 | tf_op jit(solution)/shard_map/ppermute | solution.py:26
  74.7 7.2 %collective-permute-start.30 = (bf16[352,384]{1,0:T(8,128)(2,1)S(1)}, bf16[352,384]{1,0:T(8,128)(2,1)S(1)}, u32[]{:S(2)}, u32[]{:S(2)}) collective-permute-start(bf16[352,384]{1,0:T(8,128)(2,1)S(1)} %copied.8.after), channel_id=1, source_target_pairs={{0,1},{1,0},{2,3},{3,2},{4,5},{5,4},{6,7},{7,6},{8,9},{9,8},{10,11... | collective-permute-start | bytes 811016 | tf_op jit(solution)/shard_map/ppermute | solution.py:26
  74.8 10.7 %collective-permute-start.17 = (bf16[352,768]{1,0:T(8,128)(2,1)S(1)}, bf16[352,768]{1,0:T(8,128)(2,1)S(1)}, u32[]{:S(2)}, u32[]{:S(2)}) collective-permute-start(bf16[352,768]{1,0:T(8,128)(2,1)S(1)} %collective-permute-done.16.array), channel_id=1, source_target_pairs={{0,1},{1,0},{2,3},{3,2},{4,5},{5,4},{6,7},{7,6},{8,9},{9,8},{10,11... | collective-permute-start | bytes 1622024 | tf_op jit(solution)/shard_map/ppermute | solution.py:26
  77.5 8.6 %collective-permute-start.23 = (bf16[352,384]{1,0:T(8,128)(2,1)S(1)}, bf16[352,384]{1,0:T(8,128)(2,1)S(1)}, u32[]{:S(2)}, u32[]{:S(2)}) collective-permute-start(bf16[352,384]{1,0:T(8,128)(2,1)S(1)} %copied.9), channel_id=1, source_target_pairs={{0,1},{1,0},{2,3},{3,2},{4,5},{5,4},{6,7},{7,6},{8,9},{9,8},{10,11... | collective-permute-start | bytes 811016 | tf_op jit(solution)/shard_map/ppermute | solution.py:26
  83.9 17.5 %collective-permute-start.31 = (bf16[352,768]{1,0:T(8,128)(2,1)}, bf16[352,768]{1,0:T(8,128)(2,1)}, u32[]{:S(2)}, u32[]{:S(2)}) collective-permute-start(bf16[352,768]{1,0:T(8,128)(2,1)} %fusion.16), channel_id=1, source_target_pairs={{0,64},{64,128},{128,192},{192,0},{1,65},{65,129},{129,193},{193,1... | collective-permute-start | bytes 1622024 | tf_op jit(solution)/shard_map/ppermute | solution.py:233
  87.3 14.0 %collective-permute-start.32 = (bf16[352,768]{1,0:T(8,128)(2,1)S(1)}, bf16[352,768]{1,0:T(8,128)(2,1)}, u32[]{:S(2)}, u32[]{:S(2)}) collective-permute-start(bf16[352,768]{1,0:T(8,128)(2,1)S(1)} %fusion.15.after), channel_id=1, source_target_pairs={{0,192},{64,0},{128,64},{192,128},{1,193},{65,1},{129,65},{193,129... | collective-permute-start | bytes 1622024 | tf_op jit(solution)/shard_map/ppermute | solution.py:233
  89.6 5.9 %collective-permute-start.27 = (bf16[352,384]{1,0:T(8,128)(2,1)}, bf16[352,384]{1,0:T(8,128)(2,1)}, u32[]{:S(2)}, u32[]{:S(2)}) collective-permute-start(bf16[352,384]{1,0:T(8,128)(2,1)} %half.7), channel_id=1, source_target_pairs={{0,2},{1,7},{2,4},{3,1},{4,6},{5,3},{6,0},{7,5},{8,10},{9,15},{10,... | collective-permute-start | bytes 811016 | tf_op jit(solution)/shard_map/ppermute | solution.py:26
  90.9 8.4 %collective-permute-start.26 = (bf16[352,768]{1,0:T(8,128)(2,1)S(1)}, bf16[352,768]{1,0:T(8,128)(2,1)S(1)}, u32[]{:S(2)}, u32[]{:S(2)}) collective-permute-start(bf16[352,768]{1,0:T(8,128)(2,1)S(1)} %collective-permute-done.25.array), channel_id=1, source_target_pairs={{0,1},{1,0},{2,3},{3,2},{4,5},{5,4},{6,7},{7,6},{8,9},{9,8},{10,11... | collective-permute-start | bytes 1622024 | tf_op jit(solution)/shard_map/ppermute | solution.py:26
  95.5 5.9 %collective-permute-start.28 = (bf16[352,384]{1,0:T(8,128)(2,1)}, bf16[352,384]{1,0:T(8,128)(2,1)S(1)}, u32[]{:S(2)}, u32[]{:S(2)}) collective-permute-start(bf16[352,384]{1,0:T(8,128)(2,1)} %collective-permute-done.27), channel_id=1, source_target_pairs={{0,1},{1,0},{2,3},{3,2},{4,5},{5,4},{6,7},{7,6},{8,9},{9,8},{10,11... | collective-permute-start | bytes 811016 | tf_op jit(solution)/shard_map/ppermute | solution.py:26
  111.5 15.3 %all-to-all-start.1 = ((bf16[32,16,96]{2,1,0:T(8,128)(2,1)}), bf16[32,16,96]{2,1,0:T(8,128)(2,1)S(1)}, u32[]{:S(2)}, u32[]{:S(2)}) async-start(bf16[32,16,96]{2,1,0:T(8,128)(2,1)} %bitcast.63), calls=%async_computation.1 | async-start | bytes 262144 | tf_op jit(solution)/shard_map/all_to_all | solution.py:337
  (31 other events, 209.5 us)
where the time goes:
time: 128 us; the launch traced here: 127 us
  starting transfers between devices  57.8 us (45%)
  waiting for transfers between devices  25.4 us (20%)
  matrix products  21.1 us (16%)
  Pallas kernels  11.1 us (9%)
  local copies, waits for them, and re-layouts  8.48 us (7%)
  other arithmetic  2.8 us (2%)
    ppermute x30, starting transfers between devices, move(): return lax.ppermute(array, 'mp', pairs)  35.5 us
    dot_general x20, matrix products, product(): total = total + jnp.dot(part, weight, preferred_element_type=f32)  17.6 us
    ppermute x30, waiting for transfers between devices, move(): return lax.ppermute(array, 'mp', pairs)  15.9 us
    all_to_all x1, waiting for transfers between devices, on_device(): lax.all_to_all(product, 'mp', split_axis=0, concat_axis=0, tiled=True)  8.53 us
    ppermute x5, starting transfers between devices, var_shift(): return lax.ppermute(array, 'var', [(k, (k + step) % n) for k in range(n)])  7.73 us
    all_to_all x1, starting transfers between devices, on_device(): lax.all_to_all(product, 'mp', split_axis=0, concat_axis=0, tiled=True)  6.72 us
    unnamed x50, local copies, waits for them, and re-layouts  6.2 us
    all_to_all x1, starting transfers between devices, on_device(): lax.all_to_all(own, 'var', split_axis=0, concat_axis=0, tiled=True)  4.84 us
  transfers between devices with their start and end apart: 38, of which 9 were waited for; matrix products, arithmetic and copies ran while one was open for 14% of the time, Pallas kernels for 8%

commit v1 on v0

--- a/solution.py
+++ b/solution.py
@@ -264,11 +264,11 @@
     received = lax.all_to_all(own, "var", split_axis=0, concat_axis=0, tiled=True)
     groups = jnp.stack([(var_place + step) % var_count for step in STEPS]).astype(jnp.int32)
     weights = [w.reshape(-1, 2 * tile_width) for w in weights]
-    early = pack(received, groups, 0, 2, ordered)
+    early = pack(received, groups, 0, 2, out_bias)
     late = pack(received, groups, 2, 2, early)
     early = [early] + [along_z(early, step) for step in (1, 3, 2)]
     late = [late] + [along_z(late, step) for step in (1, 3, 2)]
-    early += [other_core(part) for part in early]
+    early += [other_core(copied(early[0], ordered))] + [other_core(part) for part in early[1:]]
 
     def product(line, near, far):
         total = 0.0

time: 128 us -> 128 us (level)
    pallas_call x10 -> x11, Pallas kernels: 3.6 us -> 3.62 us  [local_call(): pl.pallas_call(kernel, grid=(1,), in_specs=[pl.BlockSpec(memory_space=pl....]
  transfers between devices with their start and end apart: 38 -> 38, of which waited for: 9 -> 8; matrix products, arithmetic and copies ran while one was open for 14% -> 14% of each run, Pallas kernels for 8% -> 8%
where the time goes in v1:
time: 128 us; the launch traced here: 127 us
  starting transfers between devices  57.1 us (45%)
  waiting for transfers between devices  26 us (20%)
  matrix products  21.1 us (16%)
  Pallas kernels  11.1 us (9%)
  local copies, waits for them, and re-layouts  8.48 us (7%)
  other arithmetic  2.8 us (2%)
    ppermute x30, starting transfers between devices, move(): return lax.ppermute(array, 'mp', pairs)  35.6 us
    dot_general x20, matrix products, product(): total = total + jnp.dot(part, weight, preferred_element_type=f32)  17.6 us
    ppermute x30, waiting for transfers between devices, move(): return lax.ppermute(array, 'mp', pairs)  16.4 us
    all_to_all x1, waiting for transfers between devices, on_device(): lax.all_to_all(product, 'mp', split_axis=0, concat_axis=0, tiled=True)  8.63 us
    ppermute x5, starting transfers between devices, var_shift(): return lax.ppermute(array, 'var', [(k, (k + step) % n) for k in range(n)])  7.83 us
    unnamed x50, local copies, waits for them, and re-layouts  6.2 us
    all_to_all x1, starting transfers between devices, on_device(): lax.all_to_all(product, 'mp', split_axis=0, concat_axis=0, tiled=True)  5.8 us
    all_to_all x1, starting transfers between devices, on_device(): lax.all_to_all(own, 'var', split_axis=0, concat_axis=0, tiled=True)  4.84 us
  transfers between devices with their start and end apart: 38, of which 8 were waited for; matrix products, arithmetic and copies ran while one was open for 14% of the time, Pallas kernels for 8%

profile of v1, /device:TPU:1, one launch (start us, length us, event | category | flops | bytes accessed | tf_op | source)
XLA Modules:
  0.0 127.4 jit_solution(10350941984029306890)
XLA Ops:
  0.9 1.6 %fusion.18 = bf16[22,16,384]{2,1,0:T(8,128)(2,1)S(1)} fusion(bf16[22,16,64]{2,1,0:T(8,128)(2,1)} %param.11, bf16[22,64,384]{2,1,0:T(8,128)(2,1)} %param.12, f32[22,384]{1,0:T(8,128)S(1)} %convert_element_type.41), kind=kOutput, calls=%fused_computation.27 | convolution fusion | flops 17571840 | bytes 1430528 | tf_op jit(solution)/shard_map/vtp,vpc->vtc/dot_general | solution.py:257
  3.6 4.8 %all-to-all-start = ((bf16[4,4,88,96]{3,2,1,0:T(8,128)(2,1)}), bf16[4,4,88,96]{3,2,1,0:T(8,128)(2,1)S(1)}, u32[]{:S(2)}, u32[]{:S(2)}) async-start(bf16[4,4,88,96]{3,2,1,0:T(8,128)(2,1)} %bitcast.5), calls=%async_computation | async-start | bytes 720896 | tf_op jit(solution)/shard_map/all_to_all | solution.py:264
  9.2 1.7 %copy-done.3 = bf16[32,96,384]{2,1,0:T(8,128)(2,1)S(1)} copy-done((bf16[32,96,384]{2,1,0:T(8,128)(2,1)S(1)}, bf16[32,96,384]{2,1,0:T(8,128)(2,1)}, u32[]{:S(2)}) %copy-start.3) | copy-done | bytes 2359320
  10.8 1.7 %copy-done.4 = bf16[32,96,384]{2,1,0:T(8,128)(2,1)S(1)} copy-done((bf16[32,96,384]{2,1,0:T(8,128)(2,1)S(1)}, bf16[32,96,384]{2,1,0:T(8,128)(2,1)}, u32[]{:S(2)}) %copy-start.4) | copy-done | bytes 2359320
  12.5 4.3 %order_weights.1 = (bf16[8,96,768]{2,1,0:T(8,128)(2,1)}, bf16[8,96,768]{2,1,0:T(8,128)(2,1)}, bf16[8,96,768]{2,1,0:T(8,128)(2,1)}, bf16[4,96,768]{2,1,0:T(8,128)...) custom-call(s32[32]{0:T(128)S(1)} %fusion.31.order, bf16[32,96,384]{2,1,0:T(8,128)(2,1)S(1)} %copy-done.3, ...), custom_call_target="tpu_custom_call" | custom-call | bytes 10485760 | tf_op jit(solution)/shard_map/order_weights/pallas_call | solution.py:183
  17.6 2.0 %collective-permute-start.5 = (bf16[2,88,384]{2,1,0:T(8,128)(2,1)S(1)}, bf16[2,88,384]{2,1,0:T(8,128)(2,1)S(1)}, u32[]{:S(2)}, u32[]{:S(2)}) collective-permute-start(bf16[2,88,384]{2,1,0:T(8,128)(2,1)S(1)} %copied.7), channel_id=1, source_target_pairs={{0,1},{1,0},{2,3},{3,2},{4,5},{5,4},{6,7},{7,6},{8,9},{9,8},{10,11... | collective-permute-start | bytes 405512 | tf_op jit(solution)/shard_map/ppermute | solution.py:26
  20.3 2.7 %collective-permute-start.3 = (bf16[2,88,384]{2,1,0:T(8,128)(2,1)S(1)}, bf16[2,88,384]{2,1,0:T(8,128)(2,1)S(1)}, u32[]{:S(2)}, u32[]{:S(2)}) collective-permute-start(bf16[2,88,384]{2,1,0:T(8,128)(2,1)S(1)} %pack.2.after.array.refs_0_), channel_id=1, source_target_pairs={{0,24},{1,25},{2,26},{3,27},{4,28},{5,29},{6,30},{7,31},{8,0},{9,1... | collective-permute-start | bytes 405512 | tf_op jit(solution)/shard_map/ppermute | solution.py:26
  24.1 1.5 %collective-permute-start = (bf16[2,88,384]{2,1,0:T(8,128)(2,1)S(1)}, bf16[2,88,384]{2,1,0:T(8,128)(2,1)S(1)}, u32[]{:S(2)}, u32[]{:S(2)}) collective-permute-start(bf16[2,88,384]{2,1,0:T(8,128)(2,1)S(1)} %pack.3.refs_0_), channel_id=1, source_target_pairs={{0,8},{1,9},{2,10},{3,11},{4,12},{5,13},{6,14},{7,15},{8,16},{9,17... | collective-permute-start | bytes 405512 | tf_op jit(solution)/shard_map/ppermute | solution.py:26
  25.6 1.8 %collective-permute-start.1 = (bf16[2,88,384]{2,1,0:T(8,128)(2,1)S(1)}, bf16[2,88,384]{2,1,0:T(8,128)(2,1)S(1)}, u32[]{:S(2)}, u32[]{:S(2)}) collective-permute-start(bf16[2,88,384]{2,1,0:T(8,128)(2,1)S(1)} %pack.3.refs_0_), channel_id=1, source_target_pairs={{0,24},{1,25},{2,26},{3,27},{4,28},{5,29},{6,30},{7,31},{8,0},{9,1... | collective-permute-start | bytes 405512 | tf_op jit(solution)/shard_map/ppermute | solution.py:26
  30.0 8.7 %collective-permute-done.4.refs_3_ = bf16[2,88,384]{2,1,0:T(8,128)(2,1)S(1)} collective-permute-done((bf16[2,88,384]{2,1,0:T(8,128)(2,1)S(1)}, bf16[2,88,384]{2,1,0:T(8,128)(2,1)S(1)}, u32[]{:S(2)}, u32[]{:S(2)}) %collective-permute-start.4) | collective-permute-done | bytes 135200 | tf_op jit(solution)/shard_map/ppermute | solution.py:26
  40.6 2.8 %collective-permute-start.9 = (bf16[352,768]{1,0:T(8,128)(2,1)S(1)}, bf16[352,768]{1,0:T(8,128)(2,1)}, u32[]{:S(2)}, u32[]{:S(2)}) collective-permute-start(bf16[352,768]{1,0:T(8,128)(2,1)S(1)} %line.4.first.second), channel_id=1, source_target_pairs={{0,2},{1,7},{2,4},{3,1},{4,6},{5,3},{6,0},{7,5},{8,10},{9,15},{10,... | collective-permute-start | bytes 1622024 | tf_op jit(solution)/shard_map/ppermute | solution.py:26
  46.8 3.0 %collective-permute-done.9.array = bf16[352,768]{1,0:T(8,128)(2,1)} collective-permute-done((bf16[352,768]{1,0:T(8,128)(2,1)S(1)}, bf16[352,768]{1,0:T(8,128)(2,1)}, u32[]{:S(2)}, u32[]{:S(2)}) %collective-permute-start.9) | collective-permute-done | bytes 540704 | tf_op jit(solution)/shard_map/ppermute | solution.py:26
  49.8 2.0 %collective-permute-start.14 = (bf16[2,88,384]{2,1,0:T(8,128)(2,1)}, bf16[2,88,384]{2,1,0:T(8,128)(2,1)S(1)}, u32[]{:S(2)}, u32[]{:S(2)}) collective-permute-start(bf16[2,88,384]{2,1,0:T(8,128)(2,1)} %copy-done.9), channel_id=1, source_target_pairs={{0,1},{1,0},{2,3},{3,2},{4,5},{5,4},{6,7},{7,6},{8,9},{9,8},{10,11... | collective-permute-start | bytes 405512 | tf_op jit(solution)/shard_map/ppermute | solution.py:26
  51.8 2.0 %fusion.35 = f32[352,768]{1,0:T(8,128)S(1)} fusion(bf16[352,768]{1,0:T(8,128)(2,1)} %collective-permute-done.9.array, bf16[768,768]{1,0:T(8,128)(2,1)} %bitcast.72), kind=kOutput, calls=%fused_computation.60 | convolution fusion | flops 415236096 | bytes 2801664 | tf_op jit(solution)/shard_map/dot_general | solution.py:276
  55.0 1.8 %collective-permute-start.19 = (bf16[352,384]{1,0:T(8,128)(2,1)S(1)}, bf16[352,384]{1,0:T(8,128)(2,1)S(1)}, u32[]{:S(2)}, u32[]{:S(2)}) collective-permute-start(bf16[352,384]{1,0:T(8,128)(2,1)S(1)} %half.4.after), channel_id=1, source_target_pairs={{0,2},{1,7},{2,4},{3,1},{4,6},{5,3},{6,0},{7,5},{8,10},{9,15},{10,... | collective-permute-start | bytes 811016 | tf_op jit(solution)/shard_map/ppermute | solution.py:26
  57.5 1.6 %fusion.44 = f32[352,768]{1,0:T(8,128)S(1)} fusion(bf16[352,768]{1,0:T(8,128)(2,1)} %collective-permute-done.10.array, bf16[768,768]{1,0:T(8,128)(2,1)S(1)} %bitcast.74), kind=kOutput, calls=%fused_computation.69 | convolution fusion | flops 415236096 | bytes 2801664 | tf_op jit(solution)/shard_map/dot_general | solution.py:276
  60.3 1.6 %collective-permute-start.21 = (bf16[352,384]{1,0:T(8,128)(2,1)S(1)}, bf16[352,384]{1,0:T(8,128)(2,1)S(1)}, u32[]{:S(2)}, u32[]{:S(2)}) collective-permute-start(bf16[352,384]{1,0:T(8,128)(2,1)S(1)} %half.5.first.second), channel_id=1, source_target_pairs={{0,2},{1,7},{2,4},{3,1},{4,6},{5,3},{6,0},{7,5},{8,10},{9,15},{10,... | collective-permute-start | bytes 811016 | tf_op jit(solution)/shard_map/ppermute | solution.py:26
  62.4 1.5 %collective-permute-start.16 = (bf16[352,768]{1,0:T(8,128)(2,1)S(1)}, bf16[352,768]{1,0:T(8,128)(2,1)S(1)}, u32[]{:S(2)}, u32[]{:S(2)}) collective-permute-start(bf16[352,768]{1,0:T(8,128)(2,1)S(1)} %line.6.after), channel_id=1, source_target_pairs={{0,2},{1,7},{2,4},{3,1},{4,6},{5,3},{6,0},{7,5},{8,10},{9,15},{10,... | collective-permute-start | bytes 1622024 | tf_op jit(solution)/shard_map/ppermute | solution.py:26
  67.9 3.0 %collective-permute-start.24 = (bf16[352,768]{1,0:T(8,128)(2,1)S(1)}, bf16[352,768]{1,0:T(8,128)(2,1)S(1)}, u32[]{:S(2)}, u32[]{:S(2)}) collective-permute-start(bf16[352,768]{1,0:T(8,128)(2,1)S(1)} %fusion.17.after), channel_id=1, source_target_pairs={{0,64},{1,193},{2,66},{3,195},{4,68},{5,197},{6,70},{7,199},{8,72}... | collective-permute-start | bytes 1622024 | tf_op jit(solution)/shard_map/ppermute | solution.py:228
  72.0 2.8 %collective-permute-start.22 = (bf16[352,384]{1,0:T(8,128)(2,1)S(1)}, bf16[352,384]{1,0:T(8,128)(2,1)S(1)}, u32[]{:S(2)}, u32[]{:S(2)}) collective-permute-start(bf16[352,384]{1,0:T(8,128)(2,1)S(1)} %half.6.first.second), channel_id=1, source_target_pairs={{0,2},{1,7},{2,4},{3,1},{4,6},{5,3},{6,0},{7,5},{8,10},{9,15},{10,... | collective-permute-start | bytes 811016 | tf_op jit(solution)/shard_map/ppermute | solution.py:26
  78.3 3.9 %collective-permute-start.23 = (bf16[352,384]{1,0:T(8,128)(2,1)S(1)}, bf16[352,384]{1,0:T(8,128)(2,1)S(1)}, u32[]{:S(2)}, u32[]{:S(2)}) collective-permute-start(bf16[352,384]{1,0:T(8,128)(2,1)S(1)} %copied.11), channel_id=1, source_target_pairs={{0,1},{1,0},{2,3},{3,2},{4,5},{5,4},{6,7},{7,6},{8,9},{9,8},{10,11... | collective-permute-start | bytes 811016 | tf_op jit(solution)/shard_map/ppermute | solution.py:26
  83.1 1.5 %fusion.16 = bf16[352,768]{1,0:T(8,128)(2,1)} fusion(f32[352,768]{1,0:T(8,128)S(1)} %fusion.47, f32[352,768]{1,0:T(8,128)S(1)} %fusion.46, f32[352,768]{1,0:T(8,128)S(1)} %fusion.45, f32[352,768]{1,0:T(8,128)S(1)} %fusion.44, bf16[352,768]{1,0:T(8,128)(2,1)S(1)} %line.5.after, bf16[768,768]{1,0:T(8,128)(2,1)S(1)} %bitcast.65, ...), kind=kOutput, calls=%fused_computation.24 | convolution fusion | flops 417398784 | bytes 7127041 | tf_op jit(solution)/shard_map/dot_general | solution.py:276
  84.6 1.7 %collective-permute-start.31 = (bf16[352,768]{1,0:T(8,128)(2,1)}, bf16[352,768]{1,0:T(8,128)(2,1)}, u32[]{:S(2)}, u32[]{:S(2)}) collective-permute-start(bf16[352,768]{1,0:T(8,128)(2,1)} %fusion.16), channel_id=1, source_target_pairs={{0,64},{64,128},{128,192},{192,0},{1,65},{65,129},{129,193},{193,1... | collective-permute-start | bytes 1622024 | tf_op jit(solution)/shard_map/ppermute | solution.py:233
  92.1 1.9 %fusion.41 = f32[352,768]{1,0:T(8,128)S(1)} fusion(bf16[352,768]{1,0:T(8,128)(2,1)S(1)} %collective-permute-done.25.array, bf16[768,768]{1,0:T(8,128)(2,1)} %bitcast.73), kind=kOutput, calls=%fused_computation.66 | convolution fusion | flops 415236096 | bytes 2801664 | tf_op jit(solution)/shard_map/dot_general | solution.py:276
  94.0 2.3 %collective-permute-done.27 = bf16[352,384]{1,0:T(8,128)(2,1)} collective-permute-done((bf16[352,384]{1,0:T(8,128)(2,1)}, bf16[352,384]{1,0:T(8,128)(2,1)}, u32[]{:S(2)}, u32[]{:S(2)}) %collective-permute-start.27) | collective-permute-done | bytes 270368 | tf_op jit(solution)/shard_map/ppermute | solution.py:26
  96.3 2.4 %collective-permute-start.28 = (bf16[352,384]{1,0:T(8,128)(2,1)}, bf16[352,384]{1,0:T(8,128)(2,1)S(1)}, u32[]{:S(2)}, u32[]{:S(2)}) collective-permute-start(bf16[352,384]{1,0:T(8,128)(2,1)} %collective-permute-done.27), channel_id=1, source_target_pairs={{0,1},{1,0},{2,3},{3,2},{4,5},{5,4},{6,7},{7,6},{8,9},{9,8},{10,11... | collective-permute-start | bytes 811016 | tf_op jit(solution)/shard_map/ppermute | solution.py:26
  98.6 1.4 %fusion.43 = f32[352,768]{1,0:T(8,128)S(1)} fusion(bf16[352,384]{1,0:T(8,128)(2,1)} %collective-permute-done.27, bf16[384,768]{1,0:T(8,128)(2,1)S(1)} %bitcast.83), kind=kOutput, calls=%fused_computation.68 | convolution fusion | flops 207618048 | bytes 1941504 | tf_op jit(solution)/shard_map/dot_general | solution.py:276
  102.5 1.7 %fusion.5 = f32[352,768]{1,0:T(8,128)S(1)} fusion(f32[352,768]{1,0:T(8,128)S(1)} %fusion.7, bf16[352,384]{1,0:T(8,128)(2,1)S(1)} %collective-permute-done.28, bf16[384,768]{1,0:T(8,128)(2,1)S(1)} %bitcast.79, bf16[352,768]{1,0:T(8,128)(2,1)} %collective-permute-done.32, bf16[352,768]{1,0:T(8,128)(2,1)} %collective-permute-done.31), kind=kOutput, calls=%fused_computation.8 | convolution fusion | flops 208969728 | bytes 4104192 | tf_op jit(solution)/shard_map/dot_general | solution.py:276
  105.2 2.1 %collective-permute-start.33 = (bf16[4,384]{1,0:T(4,128)(2,1)S(1)}, bf16[4,384]{1,0:T(4,128)(2,1)S(1)}, u32[]{:S(2)}, u32[]{:S(2)}) collective-permute-start(bf16[4,384]{1,0:T(4,128)(2,1)S(1)} %convolution_convert_fusion.1), channel_id=1, source_target_pairs={{0,128},{64,192},{128,0},{192,64},{1,129},{65,193},{129,1},{193,65... | collective-permute-start | bytes 9224 | tf_op jit(solution)/shard_map/ppermute | solution.py:233
  108.0 2.0 %collective-permute-start.35 = (bf16[4,384]{1,0:T(4,128)(2,1)S(1)}, bf16[4,384]{1,0:T(4,128)(2,1)S(1)}, u32[]{:S(2)}, u32[]{:S(2)}) collective-permute-start(bf16[4,384]{1,0:T(4,128)(2,1)S(1)} %convolution_convert_fusion.1), channel_id=1, source_target_pairs={{0,192},{64,0},{128,64},{192,128},{1,193},{65,1},{129,65},{193,129... | collective-permute-start | bytes 9224 | tf_op jit(solution)/shard_map/ppermute | solution.py:233
  112.3 5.8 %all-to-all-start.1 = ((bf16[32,16,96]{2,1,0:T(8,128)(2,1)}), bf16[32,16,96]{2,1,0:T(8,128)(2,1)S(1)}, u32[]{:S(2)}, u32[]{:S(2)}) async-start(bf16[32,16,96]{2,1,0:T(8,128)(2,1)} %bitcast.63), calls=%async_computation.1 | async-start | bytes 262144 | tf_op jit(solution)/shard_map/all_to_all | solution.py:337
  118.1 8.6 %all-to-all-done.1 = bf16[32,16,96]{2,1,0:T(8,128)(2,1)S(1)} async-done(((bf16[32,16,96]{2,1,0:T(8,128)(2,1)}), bf16[32,16,96]{2,1,0:T(8,128)(2,1)S(1)}, u32[]{:S(2)}, u32[]{:S(2)}) %all-to-all-start.1) | async-done | bytes 98336 | tf_op jit(solution)/shard_map/all_to_all | solution.py:337
  (158 shorter events, 38.4 us)
Async XLA Ops:
  3.6 13.2 %all-to-all-start = ((bf16[4,4,88,96]{3,2,1,0:T(8,128)(2,1)}), bf16[4,4,88,96]{3,2,1,0:T(8,128)(2,1)S(1)}, u32[]{:S(2)}, u32[]{:S(2)}) async-start(bf16[4,4,88,96]{3,2,1,0:T(8,128)(2,1)} %bitcast.5), calls=%async_computation | async-start | bytes 720896 | tf_op jit(solution)/shard_map/all_to_all | solution.py:264
  17.6 8.0 %collective-permute-start.5 = (bf16[2,88,384]{2,1,0:T(8,128)(2,1)S(1)}, bf16[2,88,384]{2,1,0:T(8,128)(2,1)S(1)}, u32[]{:S(2)}, u32[]{:S(2)}) collective-permute-start(bf16[2,88,384]{2,1,0:T(8,128)(2,1)S(1)} %copied.7), channel_id=1, source_target_pairs={{0,1},{1,0},{2,3},{3,2},{4,5},{5,4},{6,7},{7,6},{8,9},{9,8},{10,11... | collective-permute-start | bytes 405512 | tf_op jit(solution)/shard_map/ppermute | solution.py:26
  19.6 7.8 %collective-permute-start.2 = (bf16[2,88,384]{2,1,0:T(8,128)(2,1)S(1)}, bf16[2,88,384]{2,1,0:T(8,128)(2,1)S(1)}, u32[]{:S(2)}, u32[]{:S(2)}) collective-permute-start(bf16[2,88,384]{2,1,0:T(8,128)(2,1)S(1)} %pack.2.after.array.refs_0_), channel_id=1, source_target_pairs={{0,8},{1,9},{2,10},{3,11},{4,12},{5,13},{6,14},{7,15},{8,16},{9,17... | collective-permute-start | bytes 405512 | tf_op jit(solution)/shard_map/ppermute | solution.py:26
  20.3 8.4 %collective-permute-start.3 = (bf16[2,88,384]{2,1,0:T(8,128)(2,1)S(1)}, bf16[2,88,384]{2,1,0:T(8,128)(2,1)S(1)}, u32[]{:S(2)}, u32[]{:S(2)}) collective-permute-start(bf16[2,88,384]{2,1,0:T(8,128)(2,1)S(1)} %pack.2.after.array.refs_0_), channel_id=1, source_target_pairs={{0,24},{1,25},{2,26},{3,27},{4,28},{5,29},{6,30},{7,31},{8,0},{9,1... | collective-permute-start | bytes 405512 | tf_op jit(solution)/shard_map/ppermute | solution.py:26
  23.0 15.7 %collective-permute-start.4 = (bf16[2,88,384]{2,1,0:T(8,128)(2,1)S(1)}, bf16[2,88,384]{2,1,0:T(8,128)(2,1)S(1)}, u32[]{:S(2)}, u32[]{:S(2)}) collective-permute-start(bf16[2,88,384]{2,1,0:T(8,128)(2,1)S(1)} %pack.2.after.array.refs_0_), channel_id=1, source_target_pairs={{0,16},{1,17},{2,18},{3,19},{4,20},{5,21},{6,22},{7,23},{8,24},{9,... | collective-permute-start | bytes 405512 | tf_op jit(solution)/shard_map/ppermute | solution.py:26
  24.1 15.1 %collective-permute-start = (bf16[2,88,384]{2,1,0:T(8,128)(2,1)S(1)}, bf16[2,88,384]{2,1,0:T(8,128)(2,1)S(1)}, u32[]{:S(2)}, u32[]{:S(2)}) collective-permute-start(bf16[2,88,384]{2,1,0:T(8,128)(2,1)S(1)} %pack.3.refs_0_), channel_id=1, source_target_pairs={{0,8},{1,9},{2,10},{3,11},{4,12},{5,13},{6,14},{7,15},{8,16},{9,17... | collective-permute-start | bytes 405512 | tf_op jit(solution)/shard_map/ppermute | solution.py:26
  25.6 13.6 %collective-permute-start.1 = (bf16[2,88,384]{2,1,0:T(8,128)(2,1)S(1)}, bf16[2,88,384]{2,1,0:T(8,128)(2,1)S(1)}, u32[]{:S(2)}, u32[]{:S(2)}) collective-permute-start(bf16[2,88,384]{2,1,0:T(8,128)(2,1)S(1)} %pack.3.refs_0_), channel_id=1, source_target_pairs={{0,24},{1,25},{2,26},{3,27},{4,28},{5,29},{6,30},{7,31},{8,0},{9,1... | collective-permute-start | bytes 405512 | tf_op jit(solution)/shard_map/ppermute | solution.py:26
  27.4 11.8 %collective-permute-start.6 = (bf16[2,88,384]{2,1,0:T(8,128)(2,1)S(1)}, bf16[2,88,384]{2,1,0:T(8,128)(2,1)S(1)}, u32[]{:S(2)}, u32[]{:S(2)}) collective-permute-start(bf16[2,88,384]{2,1,0:T(8,128)(2,1)S(1)} %collective-permute-done.2.refs_1_), channel_id=1, source_target_pairs={{0,1},{1,0},{2,3},{3,2},{4,5},{5,4},{6,7},{7,6},{8,9},{9,8},{10,11... | collective-permute-start | bytes 405512 | tf_op jit(solution)/shard_map/ppermute | solution.py:26
  28.7 10.5 %collective-permute-start.7 = (bf16[2,88,384]{2,1,0:T(8,128)(2,1)S(1)}, bf16[2,88,384]{2,1,0:T(8,128)(2,1)S(1)}, u32[]{:S(2)}, u32[]{:S(2)}) collective-permute-start(bf16[2,88,384]{2,1,0:T(8,128)(2,1)S(1)} %collective-permute-done.3.refs_2_), channel_id=1, source_target_pairs={{0,1},{1,0},{2,3},{3,2},{4,5},{5,4},{6,7},{7,6},{8,9},{9,8},{10,11... | collective-permute-start | bytes 405512 | tf_op jit(solution)/shard_map/ppermute | solution.py:26
  40.6 9.1 %collective-permute-start.9 = (bf16[352,768]{1,0:T(8,128)(2,1)S(1)}, bf16[352,768]{1,0:T(8,128)(2,1)}, u32[]{:S(2)}, u32[]{:S(2)}) collective-permute-start(bf16[352,768]{1,0:T(8,128)(2,1)S(1)} %line.4.first.second), channel_id=1, source_target_pairs={{0,2},{1,7},{2,4},{3,1},{4,6},{5,3},{6,0},{7,5},{8,10},{9,15},{10,... | collective-permute-start | bytes 1622024 | tf_op jit(solution)/shard_map/ppermute | solution.py:26
  43.9 13.0 %collective-permute-start.10 = (bf16[352,768]{1,0:T(8,128)(2,1)S(1)}, bf16[352,768]{1,0:T(8,128)(2,1)}, u32[]{:S(2)}, u32[]{:S(2)}) collective-permute-start(bf16[352,768]{1,0:T(8,128)(2,1)S(1)} %line.5.after), channel_id=1, source_target_pairs={{0,2},{1,7},{2,4},{3,1},{4,6},{5,3},{6,0},{7,5},{8,10},{9,15},{10,... | collective-permute-start | bytes 1622024 | tf_op jit(solution)/shard_map/ppermute | solution.py:26
  44.5 10.5 %collective-permute-start.11 = (bf16[2,88,384]{2,1,0:T(8,128)(2,1)}, bf16[2,88,384]{2,1,0:T(8,128)(2,1)S(1)}, u32[]{:S(2)}, u32[]{:S(2)}) collective-permute-start(bf16[2,88,384]{2,1,0:T(8,128)(2,1)} %copy-done.5), channel_id=1, source_target_pairs={{0,16},{1,17},{2,18},{3,19},{4,20},{5,21},{6,22},{7,23},{8,24},{9,... | collective-permute-start | bytes 405512 | tf_op jit(solution)/shard_map/ppermute | solution.py:26
  45.8 10.9 %collective-permute-start.12 = (bf16[2,88,384]{2,1,0:T(8,128)(2,1)}, bf16[2,88,384]{2,1,0:T(8,128)(2,1)S(1)}, u32[]{:S(2)}, u32[]{:S(2)}) collective-permute-start(bf16[2,88,384]{2,1,0:T(8,128)(2,1)} %copy-done.5), channel_id=1, source_target_pairs={{0,1},{1,0},{2,3},{3,2},{4,5},{5,4},{6,7},{7,6},{8,9},{9,8},{10,11... | collective-permute-start | bytes 405512 | tf_op jit(solution)/shard_map/ppermute | solution.py:26
  46.8 13.6 %collective-permute-start.13 = (bf16[2,88,384]{2,1,0:T(8,128)(2,1)}, bf16[2,88,384]{2,1,0:T(8,128)(2,1)S(1)}, u32[]{:S(2)}, u32[]{:S(2)}) collective-permute-start(bf16[2,88,384]{2,1,0:T(8,128)(2,1)} %copy-done.7), channel_id=1, source_target_pairs={{0,1},{1,0},{2,3},{3,2},{4,5},{5,4},{6,7},{7,6},{8,9},{9,8},{10,11... | collective-permute-start | bytes 405512 | tf_op jit(solution)/shard_map/ppermute | solution.py:26
  49.8 12.2 %collective-permute-start.14 = (bf16[2,88,384]{2,1,0:T(8,128)(2,1)}, bf16[2,88,384]{2,1,0:T(8,128)(2,1)S(1)}, u32[]{:S(2)}, u32[]{:S(2)}) collective-permute-start(bf16[2,88,384]{2,1,0:T(8,128)(2,1)} %copy-done.9), channel_id=1, source_target_pairs={{0,1},{1,0},{2,3},{3,2},{4,5},{5,4},{6,7},{7,6},{8,9},{9,8},{10,11... | collective-permute-start | bytes 405512 | tf_op jit(solution)/shard_map/ppermute | solution.py:26
  55.0 9.0 %collective-permute-start.19 = (bf16[352,384]{1,0:T(8,128)(2,1)S(1)}, bf16[352,384]{1,0:T(8,128)(2,1)S(1)}, u32[]{:S(2)}, u32[]{:S(2)}) collective-permute-start(bf16[352,384]{1,0:T(8,128)(2,1)S(1)} %half.4.after), channel_id=1, source_target_pairs={{0,2},{1,7},{2,4},{3,1},{4,6},{5,3},{6,0},{7,5},{8,10},{9,15},{10,... | collective-permute-start | bytes 811016 | tf_op jit(solution)/shard_map/ppermute | solution.py:26
  56.9 7.7 %collective-permute-start.18 = (bf16[352,768]{1,0:T(8,128)(2,1)}, bf16[352,768]{1,0:T(8,128)(2,1)S(1)}, u32[]{:S(2)}, u32[]{:S(2)}) collective-permute-start(bf16[352,768]{1,0:T(8,128)(2,1)} %collective-permute-done.9.array), channel_id=1, source_target_pairs={{0,1},{1,0},{2,3},{3,2},{4,5},{5,4},{6,7},{7,6},{8,9},{9,8},{10,11... | collective-permute-start | bytes 1622024 | tf_op jit(solution)/shard_map/ppermute | solution.py:26
  60.3 15.0 %collective-permute-start.21 = (bf16[352,384]{1,0:T(8,128)(2,1)S(1)}, bf16[352,384]{1,0:T(8,128)(2,1)S(1)}, u32[]{:S(2)}, u32[]{:S(2)}) collective-permute-start(bf16[352,384]{1,0:T(8,128)(2,1)S(1)} %half.5.first.second), channel_id=1, source_target_pairs={{0,2},{1,7},{2,4},{3,1},{4,6},{5,3},{6,0},{7,5},{8,10},{9,15},{10,... | collective-permute-start | bytes 811016 | tf_op jit(solution)/shard_map/ppermute | solution.py:26
  61.9 9.0 %collective-permute-start.29 = (bf16[352,768]{1,0:T(8,128)(2,1)}, bf16[352,768]{1,0:T(8,128)(2,1)S(1)}, u32[]{:S(2)}, u32[]{:S(2)}) collective-permute-start(bf16[352,768]{1,0:T(8,128)(2,1)} %collective-permute-done.10.array), channel_id=1, source_target_pairs={{0,1},{1,0},{2,3},{3,2},{4,5},{5,4},{6,7},{7,6},{8,9},{9,8},{10,11... | collective-permute-start | bytes 1622024 | tf_op jit(solution)/shard_map/ppermute | solution.py:26
  62.4 9.4 %collective-permute-start.16 = (bf16[352,768]{1,0:T(8,128)(2,1)S(1)}, bf16[352,768]{1,0:T(8,128)(2,1)S(1)}, u32[]{:S(2)}, u32[]{:S(2)}) collective-permute-start(bf16[352,768]{1,0:T(8,128)(2,1)S(1)} %line.6.after), channel_id=1, source_target_pairs={{0,2},{1,7},{2,4},{3,1},{4,6},{5,3},{6,0},{7,5},{8,10},{9,15},{10,... | collective-permute-start | bytes 1622024 | tf_op jit(solution)/shard_map/ppermute | solution.py:26
  67.9 15.2 %collective-permute-start.24 = (bf16[352,768]{1,0:T(8,128)(2,1)S(1)}, bf16[352,768]{1,0:T(8,128)(2,1)S(1)}, u32[]{:S(2)}, u32[]{:S(2)}) collective-permute-start(bf16[352,768]{1,0:T(8,128)(2,1)S(1)} %fusion.17.after), channel_id=1, source_target_pairs={{0,64},{1,193},{2,66},{3,195},{4,68},{5,197},{6,70},{7,199},{8,72}... | collective-permute-start | bytes 1622024 | tf_op jit(solution)/shard_map/ppermute | solution.py:228
  72.0 6.2 %collective-permute-start.22 = (bf16[352,384]{1,0:T(8,128)(2,1)S(1)}, bf16[352,384]{1,0:T(8,128)(2,1)S(1)}, u32[]{:S(2)}, u32[]{:S(2)}) collective-permute-start(bf16[352,384]{1,0:T(8,128)(2,1)S(1)} %half.6.first.second), channel_id=1, source_target_pairs={{0,2},{1,7},{2,4},{3,1},{4,6},{5,3},{6,0},{7,5},{8,10},{9,15},{10,... | collective-permute-start | bytes 811016 | tf_op jit(solution)/shard_map/ppermute | solution.py:26
  75.2 14.2 %collective-permute-start.25 = (bf16[352,768]{1,0:T(8,128)(2,1)S(1)}, bf16[352,768]{1,0:T(8,128)(2,1)S(1)}, u32[]{:S(2)}, u32[]{:S(2)}) collective-permute-start(bf16[352,768]{1,0:T(8,128)(2,1)S(1)} %line.7.after), channel_id=1, source_target_pairs={{0,2},{1,7},{2,4},{3,1},{4,6},{5,3},{6,0},{7,5},{8,10},{9,15},{10,... | collective-permute-start | bytes 1622024 | tf_op jit(solution)/shard_map/ppermute | solution.py:26
  75.5 7.2 %collective-permute-start.30 = (bf16[352,384]{1,0:T(8,128)(2,1)S(1)}, bf16[352,384]{1,0:T(8,128)(2,1)S(1)}, u32[]{:S(2)}, u32[]{:S(2)}) collective-permute-start(bf16[352,384]{1,0:T(8,128)(2,1)S(1)} %copied.10.after), channel_id=1, source_target_pairs={{0,1},{1,0},{2,3},{3,2},{4,5},{5,4},{6,7},{7,6},{8,9},{9,8},{10,11... | collective-permute-start | bytes 811016 | tf_op jit(solution)/shard_map/ppermute | solution.py:26
  75.6 10.8 %collective-permute-start.17 = (bf16[352,768]{1,0:T(8,128)(2,1)S(1)}, bf16[352,768]{1,0:T(8,128)(2,1)S(1)}, u32[]{:S(2)}, u32[]{:S(2)}) collective-permute-start(bf16[352,768]{1,0:T(8,128)(2,1)S(1)} %collective-permute-done.16.array), channel_id=1, source_target_pairs={{0,1},{1,0},{2,3},{3,2},{4,5},{5,4},{6,7},{7,6},{8,9},{9,8},{10,11... | collective-permute-start | bytes 1622024 | tf_op jit(solution)/shard_map/ppermute | solution.py:26
  78.3 8.7 %collective-permute-start.23 = (bf16[352,384]{1,0:T(8,128)(2,1)S(1)}, bf16[352,384]{1,0:T(8,128)(2,1)S(1)}, u32[]{:S(2)}, u32[]{:S(2)}) collective-permute-start(bf16[352,384]{1,0:T(8,128)(2,1)S(1)} %copied.11), channel_id=1, source_target_pairs={{0,1},{1,0},{2,3},{3,2},{4,5},{5,4},{6,7},{7,6},{8,9},{9,8},{10,11... | collective-permute-start | bytes 811016 | tf_op jit(solution)/shard_map/ppermute | solution.py:26
  84.6 17.5 %collective-permute-start.31 = (bf16[352,768]{1,0:T(8,128)(2,1)}, bf16[352,768]{1,0:T(8,128)(2,1)}, u32[]{:S(2)}, u32[]{:S(2)}) collective-permute-start(bf16[352,768]{1,0:T(8,128)(2,1)} %fusion.16), channel_id=1, source_target_pairs={{0,64},{64,128},{128,192},{192,0},{1,65},{65,129},{129,193},{193,1... | collective-permute-start | bytes 1622024 | tf_op jit(solution)/shard_map/ppermute | solution.py:233
  88.2 14.0 %collective-permute-start.32 = (bf16[352,768]{1,0:T(8,128)(2,1)S(1)}, bf16[352,768]{1,0:T(8,128)(2,1)}, u32[]{:S(2)}, u32[]{:S(2)}) collective-permute-start(bf16[352,768]{1,0:T(8,128)(2,1)S(1)} %fusion.15.after), channel_id=1, source_target_pairs={{0,192},{64,0},{128,64},{192,128},{1,193},{65,1},{129,65},{193,129... | collective-permute-start | bytes 1622024 | tf_op jit(solution)/shard_map/ppermute | solution.py:233
  90.4 5.9 %collective-permute-start.27 = (bf16[352,384]{1,0:T(8,128)(2,1)}, bf16[352,384]{1,0:T(8,128)(2,1)}, u32[]{:S(2)}, u32[]{:S(2)}) collective-permute-start(bf16[352,384]{1,0:T(8,128)(2,1)} %half.7), channel_id=1, source_target_pairs={{0,2},{1,7},{2,4},{3,1},{4,6},{5,3},{6,0},{7,5},{8,10},{9,15},{10,... | collective-permute-start | bytes 811016 | tf_op jit(solution)/shard_map/ppermute | solution.py:26
  91.7 8.4 %collective-permute-start.26 = (bf16[352,768]{1,0:T(8,128)(2,1)S(1)}, bf16[352,768]{1,0:T(8,128)(2,1)S(1)}, u32[]{:S(2)}, u32[]{:S(2)}) collective-permute-start(bf16[352,768]{1,0:T(8,128)(2,1)S(1)} %collective-permute-done.25.array), channel_id=1, source_target_pairs={{0,1},{1,0},{2,3},{3,2},{4,5},{5,4},{6,7},{7,6},{8,9},{9,8},{10,11... | collective-permute-start | bytes 1622024 | tf_op jit(solution)/shard_map/ppermute | solution.py:26
  96.3 5.8 %collective-permute-start.28 = (bf16[352,384]{1,0:T(8,128)(2,1)}, bf16[352,384]{1,0:T(8,128)(2,1)S(1)}, u32[]{:S(2)}, u32[]{:S(2)}) collective-permute-start(bf16[352,384]{1,0:T(8,128)(2,1)} %collective-permute-done.27), channel_id=1, source_target_pairs={{0,1},{1,0},{2,3},{3,2},{4,5},{5,4},{6,7},{7,6},{8,9},{9,8},{10,11... | collective-permute-start | bytes 811016 | tf_op jit(solution)/shard_map/ppermute | solution.py:26
  112.3 14.5 %all-to-all-start.1 = ((bf16[32,16,96]{2,1,0:T(8,128)(2,1)}), bf16[32,16,96]{2,1,0:T(8,128)(2,1)S(1)}, u32[]{:S(2)}, u32[]{:S(2)}) async-start(bf16[32,16,96]{2,1,0:T(8,128)(2,1)} %bitcast.63), calls=%async_computation.1 | async-start | bytes 262144 | tf_op jit(solution)/shard_map/all_to_all | solution.py:337
  (31 other events, 208.7 us)
